TPU v7x, 256 devices: a whole 4x4x8 slice. The times are simulated.
256 devices in a mesh: section: 64 (over y_hi, x, z), dp: 4 (over y_lo, core).
Axes of the slice: x: 4, y: 4 (y_hi: 2, y_lo: 2; y = y_hi * 2 + y_lo), z: 8, core: 2. Of those that a mesh axis runs over, the one named last changes fastest.
Arguments:
- states: bfloat16 [64, 16, 32, 2688], P('section', None, 'dp'), may hold values from -6 to 6
- inject: bfloat16 [16, 32, 2688], P(None, 'dp'), may hold values from -6 to 6
- final_cotangent: bfloat16 [16, 32, 2688], P(None, 'dp'), may hold values from -6 to 6
- weight: bfloat16 [2688, 2688], P('dp'), may hold values from -0.125 to 0.125
- norm_gain: float32 [2688], replicated, may hold values from 0.1 to 1.9
Outputs:
- d_inject: float32 [16, 32, 2688], P(None, 'dp', 'section')
- d_weight: float32 [2688, 2688], P('section', 'dp')
- d_gain: float32 [2688], replicated
All inputs are finite; a program needn't handle non-finite values.
Results may differ from a plain program's by a relative error of at most 0.018.
Values may be sent and summed in bfloat16 or wider, within the bound.
No kernel may reach another device: no remote copies, remote signals or barrier semaphores. Data moves between devices by JAX's collectives and lax.ppermute only.
A program may use at most 128 MiB of HBM per device.

v0:
```python
import math

import jax
import jax.numpy as jnp
from jax import lax
from jax.sharding import PartitionSpec as P

EPSILON = 1e-06


def from_behind(value, axis, steps):
    count = lax.axis_size(axis)
    leading, last = (max(0, -steps), min(count, count - steps))
    return lax.ppermute(value, axis, [(source, source + steps) for source in range(leading, last)])


def per_device(states, inject, final_cotangent, weight, norm_gain):
    sections = lax.axis_size("section")
    section_index = lax.axis_index("section")
    micro_count, row_count, model_width = inject.shape
    branch_scale = 1.0 / math.sqrt(sections)
    full_weight = lax.all_gather(weight, "dp", axis=0, tiled=True)
    mixed_input = states[0].astype(jnp.float32) + inject.astype(jnp.float32)
    inverse_rms = lax.rsqrt(jnp.mean(mixed_input * mixed_input, axis=-1, keepdims=True) + EPSILON)
    normed = (mixed_input * inverse_rms * norm_gain).astype(jnp.bfloat16)
    hidden = jnp.dot(
        normed.reshape(-1, model_width), full_weight, preferred_element_type=jnp.float32
    )
    hidden = hidden.reshape(micro_count, row_count, model_width)
    sigmoid_h = jax.nn.sigmoid(hidden)
    branch_slope = sigmoid_h * (1.0 + hidden * (1.0 - sigmoid_h)) * branch_scale
    turn_count = micro_count + sections - 1

    def advance(turn_index, state_carry):
        outgoing, hidden_store, input_store, gain_store = state_carry
        arrived = from_behind(outgoing, "section", -1)
        micro_slot = turn_index - (sections - 1 - section_index)
        active = jnp.logical_and(micro_slot >= 0, micro_slot < micro_count)
        micro_slot = jnp.clip(micro_slot, 0, micro_count - 1)

        def working(incoming):
            seed_block = lax.dynamic_index_in_dim(final_cotangent, micro_slot, 0, keepdims=False)
            upstream = jnp.where(section_index == sections - 1, seed_block, incoming)
            upstream_wide = upstream.astype(jnp.float32)
            slope_rows = lax.dynamic_index_in_dim(branch_slope, micro_slot, 0, keepdims=False)
            input_rows = lax.dynamic_index_in_dim(mixed_input, micro_slot, 0, keepdims=False)
            rms_rows = lax.dynamic_index_in_dim(inverse_rms, micro_slot, 0, keepdims=False)
            hidden_grad = (upstream_wide * slope_rows).astype(jnp.bfloat16)
            normed_grad = lax.dot_general(
                hidden_grad,
                full_weight,
                (((1,), (1,)), ((), ())),
                preferred_element_type=jnp.float32,
            )
            scaled_grad = normed_grad * norm_gain
            input_grad = rms_rows * (
                scaled_grad
                - input_rows
                * rms_rows
                * rms_rows
                * jnp.mean(scaled_grad * input_rows, axis=-1, keepdims=True)
            )
            passed = (upstream_wide + input_grad).astype(jnp.bfloat16)
            new_hidden = lax.dynamic_update_index_in_dim(hidden_store, hidden_grad, micro_slot, 0)
            new_input = lax.dynamic_update_index_in_dim(input_store, input_grad, micro_slot, 0)
            new_gain = gain_store + jnp.sum(normed_grad * input_rows * rms_rows, axis=0)
            return (passed, new_hidden, new_input, new_gain)

        def resting(incoming):
            return (outgoing, hidden_store, input_store, gain_store)

        return lax.cond(active, working, resting, arrived)

    initial = (
        jnp.zeros((row_count, model_width), jnp.bfloat16),
        jnp.zeros((micro_count, row_count, model_width), jnp.bfloat16),
        jnp.zeros((micro_count, row_count, model_width), jnp.float32),
        jnp.zeros((model_width,), jnp.float32),
    )
    outgoing, hidden_keep, input_keep, gain_acc = lax.fori_loop(0, turn_count, advance, initial)
    d_inject = lax.psum_scatter(input_keep, "section", scatter_dimension=2, tiled=True)
    column_width = full_weight.shape[1] // lax.axis_size("dp")
    normed_all_rows, grad_every = (
        lax.all_gather(normed, "dp", axis=1, tiled=True),
        lax.all_gather(hidden_keep, "dp", axis=1, tiled=True),
    )
    grad_cols = lax.dynamic_slice_in_dim(
        grad_every, lax.axis_index("dp") * column_width, column_width, 2
    )
    normed_flat = normed_all_rows.reshape(-1, model_width)
    grad_flat = grad_cols.reshape(-1, column_width)
    d_weight = lax.psum_scatter(
        lax.dot_general(
            normed_flat, grad_flat, (((0,), (0,)), ((), ())), preferred_element_type=jnp.float32
        ),
        "section",
        scatter_dimension=0,
        tiled=True,
    )
    d_gain = lax.psum(gain_acc, ("section", "dp"))
    return (d_inject, d_weight, d_gain)


def solution(mesh):
    in_specs = (
        P("section", None, "dp", None),
        P(None, "dp", None),
        P(None, "dp", None),
        P("dp", None),
        P(),
    )
    out_specs = (P(None, "dp", "section"), P("section", "dp"), P())
    return jax.shard_map(
        per_device, mesh=mesh, in_specs=in_specs, out_specs=out_specs, check_vma=False
    )
```

profile of v0, /device:TPU:8, one launch (start us, length us, event | category | flops | bytes accessed | tf_op | source)
XLA Modules:
  0.0 2320.1 jit_solution(4512467725862839544)
XLA Ops:
  10.0 135.3 %all-gather.4.cloned.1.call-done = bf16[2688,2688]{1,0:T(8,128)(2,1)} async-done(((bf16[672,2688]{1,0:T(8,128)(2,1)}), bf16[2688,2688]{1,0:T(8,128)(2,1)}) %all-gather.4.cloned.1.call-update) | async-done | bytes 14450704 | tf_op jit(solution)/shard_map/all_gather | solution.py:22
  154.5 1431.1 %while.20 = (s32[]{:T(128)}, bf16[8,2688]{1,0:T(8,128)(2,1)S(1)}, bf16[16,8,2688]{2,1,0:T(8,128)(2,1)S(1)}, f32[16,8,2688]{2,1,0:T(8,128)S(1)}, f32[2688]{0:T(10...) while((s32[]{:T(128)}, bf16[8,2688]{1,0:T(8,128)(2,1)S(1)}, ...), condition=%wide.region_6.7_spmd, body=%wide.region_1.6_spmd.sunk | while | flops 116164616 | bytes 15733442 | solution.py:80
  538.8 10.2 collective-permute-done
  550.3 10.2 collective-permute-done
  561.8 10.5 collective-permute-done
  573.6 10.2 collective-permute-done
  585.1 10.8 collective-permute-done
  608.6 10.6 collective-permute-done
  620.5 10.3 collective-permute-done
  643.0 10.2 collective-permute-done
  654.5 10.3 collective-permute-done
  666.1 10.3 collective-permute-done
  677.8 10.3 collective-permute-done
  689.4 534.3 %collective-permute-done = bf16[8,2688]{1,0:T(8,128)(2,1)S(1)} collective-permute-done((bf16[8,2688]{1,0:T(8,128)(2,1)S(1)}, bf16[8,2688]{1,0:T(8,128)(2,1)S(1)}, u32[]{:S(2)}, u32[]{:S(2)}) %collective-permute-start) | collective-permute-done | bytes 43040 | tf_op jit(solution)/shard_map/while/body/eval_jaxpr/ppermute | solution.py:14
  1223.7 11.7 conditional.2
  1236.7 10.3 collective-permute-done
  1247.0 11.7 conditional.2
  1270.1 11.7 conditional.2
  1283.1 10.6 collective-permute-done
  1293.7 11.7 conditional.2
  1306.7 10.3 collective-permute-done
  1317.0 11.7 conditional.2
  1330.0 10.1 collective-permute-done
  1340.1 11.7 conditional.2
  1353.1 10.5 collective-permute-done
  1363.6 11.7 conditional.2
  1376.6 10.4 collective-permute-done
  1387.0 11.7 conditional.2
  1410.0 11.7 conditional.2
  1423.0 10.6 collective-permute-done
  1433.6 11.7 conditional.2
  1446.6 10.4 collective-permute-done
  1457.0 11.7 conditional.2
  1470.0 10.3 collective-permute-done
  1480.3 11.7 conditional.2
  1493.3 10.4 collective-permute-done
  1503.7 11.7 conditional.2
  1516.7 11.2 collective-permute-done
  1527.9 11.7 conditional.2
  1540.9 10.1 collective-permute-done
  1551.0 11.7 conditional.2
  1573.9 11.7 conditional.2
  1587.1 27.1 %all-gather.8.cloned.1.call-done = bf16[16,32,2688]{2,1,0:T(8,128)(2,1)} async-done(((bf16[16,8,2688]{2,1,0:T(8,128)(2,1)}), bf16[16,32,2688]{2,1,0:T(8,128)(2,1)}) %all-gather.8.cloned.1.call-update) | async-done | bytes 2752528 | tf_op jit(solution)/shard_map/all_gather | solution.py:85
  1621.8 220.5 %fusion = f32[48,672]{1,0:T(8,128)S(1)} fusion(f32[2688,672]{1,0:T(8,128)} %convolution_bitcast_fusion), kind=kCustom, calls=%all-reduce-scatter | all-reduce-scatter fusion | flops 2064385 | bytes 7355392
  1850.4 13.4 collective-permute-start.6
  1863.8 10.6 collective-permute-start.7
  1876.4 74.7 %psum.7 = f32[2688]{0:T(1024)} all-reduce(f32[2688]{0:T(1024)S(1)} %get-tuple-element.349), channel_id=1, replica_groups=mesh['section'=64,'dp'=4] {'section','dp'}, use_global_device_ids=true, to_apply=%region_9.10 | all-reduce | flops 2688 | bytes 21504 | tf_op jit(solution)/shard_map/psum | solution.py:100
  1951.1 358.7 %all-reduce.5.cloned.1.call-done = f32[16,8,2688]{2,1,0:T(8,128)} async-done(((f32[16,8,2688]{2,1,0:T(8,128)}), f32[16,8,2688]{2,1,0:T(8,128)}) %all-reduce.5.cloned.1.call-update) | async-done | bytes 1376272
  (360 shorter events, 688.7 us)
Async XLA Ops:
  7.2 138.2 %all-gather.4.cloned.1.call-start = ((), (), s32[]{:S(2)}) async-start(), calls=%async_computation | async-start | bytes 18063360 | tf_op jit(solution)/shard_map/all_gather | solution.py:22
  7.9 1579.2 %all-gather.6.cloned.1.call-start = ((), (), s32[]{:S(2)}) async-start(), calls=%async_computation.1 | async-start | bytes 3440640 | tf_op jit(solution)/shard_map/all_gather | solution.py:84
  10.0 1604.2 %all-gather.8.cloned.1.call-start = ((), (), s32[]{:S(2)}) async-start(), calls=%async_computation.2 | async-start | bytes 3440640 | tf_op jit(solution)/shard_map/all_gather | solution.py:85
  272.1 8.2 collective-permute-start
  296.2 8.4 collective-permute-start
  320.4 8.2 collective-permute-start
  344.5 8.4 collective-permute-start
  368.7 8.2 collective-permute-start
  392.8 8.4 collective-permute-start
  441.0 8.4 collective-permute-start
  505.2 8.3 collective-permute-start
  529.2 8.2 collective-permute-start
  537.5 11.5 collective-permute-start
  549.0 11.5 collective-permute-start
  560.5 11.8 collective-permute-start
  572.3 11.5 collective-permute-start
  583.8 12.1 collective-permute-start
  595.9 11.4 collective-permute-start
  607.3 11.9 collective-permute-start
  619.2 11.6 collective-permute-start
  630.8 10.9 collective-permute-start
  641.7 11.5 collective-permute-start
  653.2 11.6 collective-permute-start
  664.8 11.6 collective-permute-start
  676.5 11.6 collective-permute-start
  688.1 535.5 %collective-permute-start = (bf16[8,2688]{1,0:T(8,128)(2,1)S(1)}, bf16[8,2688]{1,0:T(8,128)(2,1)S(1)}, u32[]{:S(2)}, u32[]{:S(2)}) collective-permute-start(bf16[8,2688]{1,0:T(8,128)(2,1)S(1)} %get-tuple-element.523), channel_id=1, source_target_pairs={{4,0},{8,4},{12,8},{16,12},{20,16},{24,20},{28,24},{32,28},{36,32}... | collective-permute-start | bytes 129032 | tf_op jit(solution)/shard_map/while/body/eval_jaxpr/ppermute | solution.py:14
  1235.3 11.6 collective-permute-start
  1258.7 11.4 collective-permute-start
  1281.8 11.9 collective-permute-start
  1305.4 11.6 collective-permute-start
  1328.6 11.4 collective-permute-start
  1351.8 11.8 collective-permute-start
  1375.3 11.7 collective-permute-start
  1398.7 11.3 collective-permute-start
  1421.7 11.9 collective-permute-start
  1445.3 11.7 collective-permute-start
  1468.7 11.6 collective-permute-start
  1492.0 11.7 collective-permute-start
  1515.4 12.5 collective-permute-start
  1539.6 11.5 collective-permute-start
  1562.7 11.2 collective-permute-start
  1586.5 723.2 %all-reduce.5.cloned.1.call-start = ((), (), s32[]{:S(2)}) async-start(), calls=%async_computation.3 | async-start | bytes 2752512
  1843.7 20.1 collective-permute-start.2
  1846.3 465.0 %collective-permute-start.3 = (f32[48,672]{1,0:T(8,128)S(1)}, f32[48,672]{1,0:T(8,128)S(1)}, u32[]{:S(2)}, u32[]{:S(2)}) collective-permute-start(f32[48,672]{1,0:T(8,128)S(1)} %fusion), channel_id=1, source_target_pairs={{0,12},{4,16},{8,20},{12,24},{16,28},{20,32},{24,36},{28,40},{32,4... | collective-permute-start | bytes 387080
  1847.6 463.7 %collective-permute-start.4 = (f32[48,672]{1,0:T(8,128)S(1)}, f32[48,672]{1,0:T(8,128)S(1)}, u32[]{:S(2)}, u32[]{:S(2)}) collective-permute-start(f32[48,672]{1,0:T(8,128)S(1)} %fusion), channel_id=1, source_target_pairs={{0,16},{4,20},{8,24},{12,28},{16,32},{20,36},{24,40},{28,44},{32,4... | collective-permute-start | bytes 387080
  1849.1 462.3 %collective-permute-start.5 = (f32[48,672]{1,0:T(8,128)S(1)}, f32[48,672]{1,0:T(8,128)S(1)}, u32[]{:S(2)}, u32[]{:S(2)}) collective-permute-start(f32[48,672]{1,0:T(8,128)S(1)} %fusion), channel_id=1, source_target_pairs={{0,20},{4,24},{8,28},{12,32},{16,36},{20,40},{24,44},{28,48},{32,5... | collective-permute-start | bytes 387080
  1850.4 461.0 %collective-permute-start.6 = (f32[48,672]{1,0:T(8,128)S(1)}, f32[48,672]{1,0:T(8,128)S(1)}, u32[]{:S(2)}, u32[]{:S(2)}) collective-permute-start(f32[48,672]{1,0:T(8,128)S(1)} %fusion), channel_id=1, source_target_pairs={{0,24},{4,28},{8,32},{12,36},{16,40},{20,44},{24,48},{28,52},{32,5... | collective-permute-start | bytes 387080
  1863.8 447.6 %collective-permute-start.7 = (f32[48,672]{1,0:T(8,128)S(1)}, f32[48,672]{1,0:T(8,128)S(1)}, u32[]{:S(2)}, u32[]{:S(2)}) collective-permute-start(f32[48,672]{1,0:T(8,128)S(1)} %fusion), channel_id=1, source_target_pairs={{0,28},{4,32},{8,36},{12,40},{16,44},{20,48},{24,52},{28,56},{32,6... | collective-permute-start | bytes 387080
  (50 other events, 579.5 us)
Sparse Core Ops, SparseCore 0:
  9.8 135.4 all-gather.3
  147.2 37.9 all-gather.5
  1586.6 27.5 all-gather.7
  1616.7 692.9 all-reduce.4
where the time goes:
time: 2330 us; the launch traced here: 2320 us
  waiting for transfers between devices  1660 us (71%)
  blocking collectives  295 us (13%)
  matrix products  162 us (7%)
  starting transfers between devices  133 us (6%)
  other arithmetic  31.9 us (1%)
    ppermute x79, waiting for transfers between devices, from_behind(): lax.ppermute(value, axis, [(source, source + steps) for source in range(l...  1140 us
    unnamed x13, waiting for transfers between devices  360 us
    unnamed x1, blocking collectives  221 us
    dot_general x16, matrix products, working(): lax.dot_general(hidden_grad, full_weight, (((1,), (1,)), ((), ())), prefe...  145 us
    all_gather x1, waiting for transfers between devices, per_device(): full_weight = lax.all_gather(weight, 'dp', axis=0, tiled=True)  135 us
    ppermute x79, starting transfers between devices, from_behind(): lax.ppermute(value, axis, [(source, source + steps) for source in range(l...  101 us
    psum x1, blocking collectives, per_device(): d_gain = lax.psum(gain_acc, ('section', 'dp'))  74.7 us
  transfers between devices with their start and end apart: 91, of which 83 were waited for; matrix products, arithmetic and copies ran while one was open for 18% of the time, Pallas kernels for 0%

commit v1 on v0

v1 whole, which is shorter than its diff:
```python
import functools
import math

import jax
import jax.numpy as jnp
from jax import lax
from jax.experimental import pallas as pl
from jax.experimental.pallas import tpu as pltpu
from jax.sharding import PartitionSpec as P

EPSILON = 1e-06
TOLERANCE = 2.0**-10
LANES = 128
AXES = ("section", "dp")
Y_HI, X, Z, Y_LO, CORE = 2, 4, 8, 2, 2


def flat(y, x, z, core):
    return (((y // Y_LO) * X + x) * Z + z) * 4 + (y % Y_LO) * CORE + core


PLACES = [
    (y, x, z, core)
    for y in range(Y_HI * Y_LO)
    for x in range(X)
    for z in range(Z)
    for core in range(CORE)
]


def move(value, target):
    return lax.ppermute(value, AXES, [(flat(*place), flat(*target(*place))) for place in PLACES])


def other_core(y, x, z, core):
    return (y, x, z, 1 - core)


def y_up(y, x, z, core):
    return ((y + 1) % (Y_HI * Y_LO), x, z, core)


def y_down(y, x, z, core):
    return ((y - 1) % (Y_HI * Y_LO), x, z, core)


XD_GROUPS = [
    [flat(yh * Y_LO + d // CORE, x, z, d % CORE) for x in range(X) for d in range(4)]
    for yh in range(Y_HI)
    for z in range(Z)
]
YZ_GROUPS = [
    [flat(yh * Y_LO + d // CORE, x, z, d % CORE) for yh in range(Y_HI) for z in range(Z)]
    for x in range(X)
    for d in range(4)
]


def gather_weight(weight):
    rows = weight.shape[0]
    half = rows // 2
    cuts = [0, half // 32 * 16, half]
    pieces, offsets = [weight], [(0, 0, rows)]
    pieces.append(move(weight, other_core))
    offsets.append((1, 0, rows))
    far = []
    for low, high in zip(cuts[:-1], cuts[1:]):
        far.append((move(weight[low:high], y_up), low))
        far.append((move(weight[half + low : half + high], y_down), half + low))
    for piece, low in far:
        pieces += [piece, move(piece, other_core)]
        offsets += [(2, low, piece.shape[0]), (3, low, piece.shape[0])]
    return pieces, tuple(offsets)

def solve_kernel(offsets, dim, rows, max_sweeps, tolerance, shard_ref, *refs):
    pieces = refs[:len(offsets)]
    a_ref, x_ref, q_ref, gain_ref, fc_ref = refs[len(offsets):len(offsets)+5]
    g_ref, dinj_ref, dgain_ref = refs[len(offsets)+5:len(offsets)+8]
    w, wt, slope, t, p, v, sems = refs[len(offsets)+8:]
    shard = shard_ref[0]
    shard_rows = dim // 4
    copies=[]
    for n,((flip, off, cnt), piece) in enumerate(zip(offsets, pieces)):
        at = pl.multiple_of(lax.bitwise_xor(shard, flip) * shard_rows + off, 16)
        copy = pltpu.make_async_copy(piece, w.at[pl.ds(at, cnt)], sems.at[n])
        copy.start(); copies.append(copy)
    for copy in copies: copy.wait()
    groups = rows // 8
    wide = 384 if dim % 384 == 0 else 128
    scale = (1.0/max_sweeps) ** 0.5
    for j in range(0, dim, wide):
        cols = slice(j, j+wide)
        h = jnp.dot(a_ref[...], w[:, cols], preferred_element_type=jnp.float32)
        s = jax.nn.sigmoid(h)
        sl = s*(1.0+h*(1.0-s))*scale
        slope[:, cols] = sl
        fc = fc_ref[:, cols]
        v[:, cols] = (sl*jnp.concatenate([fc]*groups,0)).astype(jnp.bfloat16)
        p[:, cols] = jnp.zeros_like(sl)
    for j in range(0, dim, LANES):
        wt[j:j+LANES, :] = w[:, j:j+LANES].T
    sub = lax.broadcasted_iota(jnp.int32, (8, LANES), 0)
    def sweep(carry):
        count, _ = carry
        macc = jnp.zeros((rows, LANES), jnp.float32)
        for j in range(0, dim, wide):
            cols = slice(j, j+wide)
            u = jnp.dot(v[...], wt[:, cols], preferred_element_type=jnp.float32)
            tt = u * gain_ref[0:1, cols]
            t[:, cols] = tt
            tx = tt * x_ref[:, cols]
            for k in range(0, wide, LANES):
                macc = macc + tx[:, k:k+LANES]
        q = q_ref[...]
        kap = q*q*q*(jnp.sum(macc, axis=1, keepdims=True) * (1.0/dim))
        dacc = jnp.zeros((8, LANES), jnp.float32)
        cacc = jnp.zeros((8, LANES), jnp.float32)
        for j in range(0, dim, LANES):
            cols = slice(j, j+LANES)
            run = None
            sums = [None]*groups
            for b in range(groups-1, -1, -1):
                rs = slice(8*b, 8*b+8)
                pn = q[rs]*t[rs, cols] - kap[rs]*x_ref[rs, cols]
                d = pn - p[rs, cols]
                p[rs, cols] = pn
                dacc = dacc + d*d
                run = pn if run is None else run + pn
                sums[b] = run
            dinj_ref[:, cols] = run
            base = fc_ref[:, cols]
            for k in (2, 4, 6):
                base = base + jnp.where(sub < 8-k, pltpu.roll(run, 8-k, 0), 0.0)
            for b in range(groups):
                rs = slice(8*b, 8*b+8)
                c = base if b == groups-1 else base + sums[b+1]
                cacc = cacc + c*c
                v[rs, cols] = (c*slope[rs, cols]).astype(jnp.bfloat16)
        dn = jnp.sum(dacc, axis=1, keepdims=True)
        cn = jnp.sum(cacc, axis=1, keepdims=True)
        open_rows = jnp.sum(jnp.where(dn <= cn*(tolerance*tolerance), 0.0, 1.0))
        return count+1, open_rows
    last, _ = lax.while_loop(lambda cr: jnp.logical_and(cr[0] < max_sweeps, cr[1] > 0.0), sweep, (jnp.int32(0), jnp.float32(1)))
    for j in range(0, dim, LANES):
        cols = slice(j, j+LANES)
        acc = jnp.zeros((8, LANES), jnp.float32)
        for b in range(groups):
            rs = slice(8*b, 8*b+8)
            acc = acc + q_ref[rs]*t[rs, cols]*x_ref[rs, cols]
        dgain_ref[:, cols] = acc / gain_ref[0:1, cols]
    for k in range(4):
        g_ref[k] = v[:, k*shard_rows:(k+1)*shard_rows]


def solve(shard, pieces, offsets, a, x, q, gain, fc, tolerance):
    rows, dim = a.shape
    n = len(pieces)
    vm = pl.BlockSpec(memory_space=pltpu.VMEM)
    f32 = jnp.float32
    return pl.pallas_call(
        functools.partial(solve_kernel, offsets, dim, rows, 64, tolerance),
        out_shape=(jax.ShapeDtypeStruct((4, rows, dim//4), jnp.bfloat16), jax.ShapeDtypeStruct((8, dim), f32), jax.ShapeDtypeStruct((8, dim), f32)),
        in_specs=[pl.BlockSpec(memory_space=pltpu.SMEM)]+[pl.BlockSpec(memory_space=pl.ANY)]*n+[vm]*5,
        out_specs=(vm,)*3,
        scratch_shapes=[pltpu.VMEM((dim,dim),jnp.bfloat16)]*2+[pltpu.VMEM((rows,dim),f32)]*3+[pltpu.VMEM((rows,dim),jnp.bfloat16), pltpu.SemaphoreType.DMA((n,))],
        compiler_params=pltpu.CompilerParams(vmem_limit_bytes=58*2**20),
    )(shard, *pieces, a, x, q, gain, fc)


def per_device(states, inject, final_cotangent, weight, norm_gain):
    micro_count, row_count, dim = inject.shape
    sections = lax.axis_size("section")
    section, shard = lax.axis_index("section"), lax.axis_index("dp")
    own = micro_count * row_count // sections
    segments, groups = 4, sections // 4
    f32, bf16 = jnp.float32, jnp.bfloat16
    pieces, offsets = gather_weight(weight)

    mine = lax.all_to_all(states[0].reshape(sections, own, dim), "section", 0, 0)
    mine = mine.reshape(segments, groups, own, dim).transpose(1, 0, 2, 3)
    inject_own = lax.dynamic_index_in_dim(inject.reshape(sections, own, dim), section, 0, keepdims=False)
    final_own = lax.dynamic_index_in_dim(final_cotangent.reshape(sections, own, dim), section, 0, keepdims=False)
    x = (mine.astype(f32) + inject_own.astype(f32)).reshape(-1, dim)
    rows = x.shape[0]
    q = lax.rsqrt(jnp.mean(x * x, axis=-1, keepdims=True) + EPSILON)
    a = (x * q * norm_gain).astype(bf16)

    a_cut = a.reshape(rows, Y_HI, X, dim // 8).transpose(2, 0, 1, 3).reshape(X, 1, rows, dim // 4)
    a_cut = jnp.broadcast_to(a_cut, (X, 4, rows, dim // 4)).reshape(16, rows, dim // 4)
    a_all = lax.all_to_all(a_cut, AXES, 0, 0, axis_index_groups=XD_GROUPS)

    g, d_inject, d_gain = solve(
        shard.astype(jnp.int32).reshape(1),
        pieces,
        offsets,
        a,
        x,
        jnp.broadcast_to(q, (rows, LANES)),
        jnp.broadcast_to(norm_gain, (8, dim)),
        jnp.tile(final_own.astype(f32), (segments, 1)),
        TOLERANCE,
    )
    d_inject = jnp.sum(d_inject.reshape(segments, own, dim), axis=0)
    d_gain = jnp.sum(d_gain, axis=0)

    d_inject_cut = d_inject.astype(bf16).reshape(own, Y_HI, X, dim // 8).transpose(2, 0, 1, 3).reshape(X, own, dim // 4)
    d_gain_cut = d_gain.astype(bf16).reshape(4, dim // 4)
    pad = jnp.zeros((X, 4, 16 - own - 4, dim // 4), bf16)
    out = jnp.concatenate(
        [
            jnp.broadcast_to(g[None], (X, 4, rows, dim // 4)),
            jnp.broadcast_to(d_inject_cut[:, None], (X, 4, own, dim // 4)),
            jnp.broadcast_to(d_gain_cut[None, None], (X, 4, 4, dim // 4)),
            pad,
        ],
        axis=2,
    ).reshape(16, rows + 16, dim // 4)
    got = lax.all_to_all(out, AXES, 0, 0, axis_index_groups=XD_GROUPS)
    block = lax.dot_general(
        a_all, got[:, :rows], (((0, 1), (0, 1)), ((), ())), preferred_element_type=f32
    )
    gain_sum = jnp.sum(got[:, rows + own : rows + own + 4].astype(f32), axis=0)
    inject_got = lax.dynamic_index_in_dim(got.reshape(X, 4, rows + 16, dim // 4), shard, 1, keepdims=False)
    inject_got = inject_got[:, rows : rows + own].reshape(X * own, 16, dim // 64).transpose(1, 0, 2)
    inject_row = jnp.pad(inject_got.reshape(16, 1, -1), ((0, 0), (0, 0), (0, dim // 4 - X * own * (dim // 64))))

    part = dim // 64
    out = jnp.concatenate(
        [
            block.reshape(16, part, dim // 4).astype(bf16),
            inject_row,
            jnp.broadcast_to(gain_sum.astype(bf16)[None], (16, 4, dim // 4)),
            jnp.zeros((16, 48 - part - 5, dim // 4), bf16),
        ],
        axis=1,
    )
    got = lax.all_to_all(out, AXES, 0, 0, axis_index_groups=YZ_GROUPS)
    total = jnp.sum(got.astype(f32), axis=0)
    d_weight = total[:part]
    d_gain = total[part + 1 : part + 5].reshape(dim)
    d_inject = got[:, part, : X * own * part].reshape(Y_HI, Z, X, own, part).transpose(0, 2, 1, 3, 4)
    d_inject = d_inject.reshape(micro_count, row_count, part).astype(f32)
    return d_inject, d_weight, d_gain


def solution(mesh):
    in_specs = (
        P("section", None, "dp", None),
        P(None, "dp", None),
        P(None, "dp", None),
        P("dp", None),
        P(),
    )
    out_specs = (P(None, "dp", "section"), P("section", "dp"), P())
    return jax.shard_map(
        per_device, mesh=mesh, in_specs=in_specs, out_specs=out_specs, check_vma=False
    )
```

time: 2330 us -> 283 us (0.12)
  waiting for transfers between devices: 1660 us -> 111 us
  blocking collectives: 295 us -> 36.8 us
  matrix products: 162 us -> 5.06 us
  starting transfers between devices: 133 us -> 37.1 us
  Pallas kernels: 0 us -> 50.5 us
    ppermute x79 -> x9, waiting for transfers between devices: 1140 us -> 45.2 us  [move(): lax.ppermute(value, AXES, [(flat(*place), flat(*target(*place))) for plac...]
    unnamed x13 -> x0, waiting for transfers between devices: 360 us -> none
    unnamed x1 -> x0, blocking collectives: 221 us -> none
    all_gather x3 -> x0, waiting for transfers between devices: 162 us -> none  [the longest x1 135 us: per_device(): full_weight = lax.all_gather(weight, 'dp', axis=0, tiled=True)]
    dot_general x18 -> x1, matrix products: 162 us -> 5.06 us  [per_device(): lax.dot_general(a_all, got[:, :rows], (((0, 1), (0, 1)), ((), ())), prefe...]
    ppermute x79 -> x9, starting transfers between devices: 101 us -> 5.68 us  [move(): lax.ppermute(value, AXES, [(flat(*place), flat(*target(*place))) for plac...]
    psum x1 -> x0, blocking collectives: 74.7 us -> none  [per_device(): d_gain = lax.psum(gain_acc, ('section', 'dp'))]
    all_to_all x0 -> x3, waiting for transfers between devices: none -> 65.4 us  [the longest x1 48 us: per_device(): got = lax.all_to_all(out, AXES, 0, 0, axis_index_groups=XD_GROUPS)]
  transfers between devices with their start and end apart: 91 -> 12, of which waited for: 83 -> 5; matrix products, arithmetic and copies ran while one was open for 18% -> 10% of each run, Pallas kernels for 0% -> 18%
where the time goes in v1:
time: 283 us; the launch traced here: 280 us
  waiting for transfers between devices  111 us (39%)
  Pallas kernels  50.5 us (18%)
  starting transfers between devices  37.1 us (13%)
  blocking collectives  36.8 us (13%)
  local copies, waits for them, and re-layouts  30.6 us (11%)
  other arithmetic  8.84 us (3%)
  matrix products  5.06 us (2%)
    pallas_call x1, Pallas kernels, solve(): pl.pallas_call(functools.partial(solve_kernel, offsets, dim, rows, 64, to...  50.5 us
    all_to_all x1, waiting for transfers between devices, per_device(): got = lax.all_to_all(out, AXES, 0, 0, axis_index_groups=XD_GROUPS)  48 us
    ppermute x9, waiting for transfers between devices, move(): lax.ppermute(value, AXES, [(flat(*place), flat(*target(*place))) for plac...  45.2 us
    all_to_all x1, blocking collectives, per_device(): got = lax.all_to_all(out, AXES, 0, 0, axis_index_groups=YZ_GROUPS)  36.8 us
    all_to_all x1, waiting for transfers between devices, per_device(): lax.all_to_all(states[0].reshape(sections, own, dim), 'section', 0, 0)  17.3 us
    all_to_all x1, starting transfers between devices, per_device(): lax.all_to_all(states[0].reshape(sections, own, dim), 'section', 0, 0)  13.8 us
    all_to_all x1, starting transfers between devices, per_device(): got = lax.all_to_all(out, AXES, 0, 0, axis_index_groups=XD_GROUPS)  12.1 us
    ppermute x9, starting transfers between devices, move(): lax.ppermute(value, AXES, [(flat(*place), flat(*target(*place))) for plac...  5.68 us
  transfers between devices with their start and end apart: 12, of which 5 were waited for; matrix products, arithmetic and copies ran while one was open for 10% of the time, Pallas kernels for 18%

profile of v1, /device:TPU:8, one launch (start us, length us, event | category | flops | bytes accessed | tf_op | source)
XLA Modules:
  0.0 280.3 jit_solution(8722790540822439223)
XLA Ops:
  0.6 2.7 reshape_squeeze.4
  3.3 13.8 %all-to-all-start = ((bf16[64,2,2688]{2,1,0:T(2,128)(2,1)}), bf16[64,2,2688]{2,1,0:T(2,128)(2,1)S(1)}, u32[]{:S(2)}, u32[]{:S(2)}) async-start(bf16[64,2,2688]{2,1,0:T(2,128)(2,1)} %reshape_squeeze.4), calls=%async_computation | async-start | bytes 1376256 | tf_op jit(solution)/shard_map/all_to_all | solution.py:179
  17.2 2.9 %fusion.12 = (bf16[176,2688]{1,0:T(8,128)(2,1)}, bf16[176,2688]{1,0:T(8,128)(2,1)}) fusion(bf16[672,2688]{1,0:T(8,128)(2,1)} %refs_0_.1), kind=kLoop, calls=%fused_computation.25 | loop fusion | bytes 3784704 | tf_op jit(solution)/shard_map/slice | solution.py:69
  20.2 2.5 collective-permute-start.5
  22.6 0.3 reshape.112
  23.0 17.3 %all-to-all-done = bf16[64,2,2688]{2,1,0:T(2,128)(2,1)S(1)} async-done(((bf16[64,2,2688]{2,1,0:T(2,128)(2,1)}), bf16[64,2,2688]{2,1,0:T(2,128)(2,1)S(1)}, u32[]{:S(2)}, u32[]{:S(2)}) %all-to-all-start) | async-done | bytes 688160 | tf_op jit(solution)/shard_map/all_to_all | solution.py:179
  40.4 1.1 copy.56
  41.6 0.2 multiply_reduce_fusion
  41.8 0.1 copy.57
  42.0 0.2 rsqrt.12
  42.1 2.2 reshape.113
  44.3 1.3 fusion.10
  45.6 1.5 copy.58
  47.2 2.0 broadcast_in_dim.23
  49.1 5.6 %all-to-all-start.1 = ((bf16[16,128,672]{1,2,0:T(8,128)(2,1)}), bf16[16,128,672]{1,2,0:T(8,128)(2,1)}, u32[]{:S(2)}, u32[]{:S(2)}) async-start(bf16[16,128,672]{1,2,0:T(8,128)(2,1)} %bitcast.33), calls=%async_computation.1 | async-start | bytes 5505024 | tf_op jit(solution)/shard_map/all_to_all | solution.py:190
  54.7 1.5 fusion.13
  56.2 0.4 collective-permute-start.1
  56.6 1.7 collective-permute-start.3
  58.3 2.7 reshape.117
  61.0 43.2 %collective-permute-done.1.refs_2_ = bf16[160,2688]{1,0:T(8,128)(2,1)} collective-permute-done((bf16[160,2688]{1,0:T(8,128)(2,1)S(1)}, bf16[160,2688]{1,0:T(8,128)(2,1)}, u32[]{:S(2)}, u32[]{:S(2)}) %collective-permute-start.1) | collective-permute-done | bytes 860192 | tf_op jit(solution)/shard_map/ppermute | solution.py:32
  104.3 0.5 collective-permute-start.4
  104.9 0.4 collective-permute-start.8
  105.3 0.7 bitcast_convert_fusion.1
  106.0 0.7 tile.10.refs_14_
  106.8 0.9 reshape.116.refs_11_
  107.8 1.2 multiply_convert_fusion.1.refs_10_
  108.9 0.6 collective-permute-done.6.refs_7_
  109.6 1.4 collective-permute-done.8.refs_9_
  110.9 0.7 broadcast_in_dim.24.refs_12_
  111.6 0.6 broadcast_in_dim.25.refs_13_
  112.3 50.5 %shard_map.76 = (bf16[4,128,672]{2,1,0:T(8,128)(2,1)}, f32[8,2688]{1,0:T(8,128)}, f32[8,2688]{1,0:T(8,128)}) custom-call(s32[1]{0:T(128)} %bitcast.6.shard_ref, bf16[672,2688]{1,0:T(8,128)(2,1)} %refs_0_.1, bf16[672,2688]{1,0:T(8,128)(2,1)} %collective-permute-done.refs_1_, bf16[160,2688]{1,0:T(8,128)(2,1)} %collective-permute-done.1.refs_2_, ...), custom_call_target="tpu_custom_call" | custom-call | tf_op jit(solution)/shard_map/pallas_call | solution.py:160
  162.8 0.9 reshape.118
  164.0 0.9 reduce_sum.50
  165.0 1.5 broadcast_in_dim.52
  166.5 2.3 maximum_maximum_fusion
  168.8 12.1 %all-to-all-start.2 = ((bf16[16,144,672]{2,1,0:T(8,128)(2,1)}), bf16[16,144,672]{2,1,0:T(8,128)(2,1)S(1)}, u32[]{:S(2)}, u32[]{:S(2)}) async-start(bf16[16,144,672]{2,1,0:T(8,128)(2,1)} %bitcast.9), calls=%async_computation.2 | async-start | bytes 7077888 | tf_op jit(solution)/shard_map/all_to_all | solution.py:218
  181.0 48.0 %all-to-all-done.2 = bf16[16,144,672]{2,1,0:T(8,128)(2,1)S(1)} async-done(((bf16[16,144,672]{2,1,0:T(8,128)(2,1)}), bf16[16,144,672]{2,1,0:T(8,128)(2,1)S(1)}, u32[]{:S(2)}, u32[]{:S(2)}) %all-to-all-start.2) | async-done | bytes 3096608 | tf_op jit(solution)/shard_map/all_to_all | solution.py:218
  229.0 5.1 %bitcast_convert_fusion = bf16[672,672]{1,0:T(8,128)(2,1)} fusion(bf16[16,128,672]{1,2,0:T(8,128)(2,1)} %all-to-all-done.1, bf16[16,144,672]{2,1,0:T(8,128)(2,1)S(1)} %all-to-all-done.2), kind=kOutput, calls=%fused_computation.8 | convolution fusion | flops 1850139648 | bytes 6801408 | tf_op jit(solution)/shard_map/dot_general | solution.py:219
  234.1 2.2 convert_element_type.87
  236.4 0.7 reshape.121
  237.1 1.4 copy.62
  238.5 1.5 reshape.130
  240.1 1.7 fusion.9
  241.8 36.8 %all_to_all.20 = bf16[16,48,672]{2,1,0:T(8,128)(2,1)S(1)} all-to-all(bf16[16,48,672]{2,1,0:T(8,128)(2,1)S(1)} %fusion.9), channel_id=1, replica_groups={{0,4,8,12,16,20,24,28,128,132,136,140,144,148,152,156},{1,5,9,13,17,21,..., dimensions={0} | all-to-all | bytes 2064384 | tf_op jit(solution)/shard_map/all_to_all | solution.py:237
  278.5 0.2 convert_reduce_fusion
  278.7 0.7 reshape.123
  279.5 0.1 reshape.128
  279.6 0.7 copy.66
  (41 shorter events, 1.3 us)
Async XLA Ops:
  3.3 19.3 %copy-start.1 = (bf16[16,8,2688]{2,1,0:T(8,128)(2,1)S(1)}, bf16[16,8,2688]{2,1,0:T(8,128)(2,1)}, u32[]{:S(2)}) copy-start(bf16[16,8,2688]{2,1,0:T(8,128)(2,1)} %param.6) | copy-start | bytes 2064388
  3.3 37.0 %all-to-all-start = ((bf16[64,2,2688]{2,1,0:T(2,128)(2,1)}), bf16[64,2,2688]{2,1,0:T(2,128)(2,1)S(1)}, u32[]{:S(2)}, u32[]{:S(2)}) async-start(bf16[64,2,2688]{2,1,0:T(2,128)(2,1)} %reshape_squeeze.4), calls=%async_computation | async-start | bytes 1376256 | tf_op jit(solution)/shard_map/all_to_all | solution.py:179
  17.1 5.8 %copy-start.3 = (f32[2688]{0:T(1024)S(1)}, f32[2688]{0:T(1024)}, u32[]{:S(2)}) copy-start(f32[2688]{0:T(1024)} %param.9) | copy-start | bytes 32260
  17.1 93.8 %collective-permute-start = (bf16[672,2688]{1,0:T(8,128)(2,1)}, bf16[672,2688]{1,0:T(8,128)(2,1)}, u32[]{:S(2)}, u32[]{:S(2)}) collective-permute-start(bf16[672,2688]{1,0:T(8,128)(2,1)} %refs_0_.1), channel_id=1, source_target_pairs={{0,1},{1,0},{4,5},{5,4},{8,9},{9,8},{12,13},{13,12},{16,17},{17,16... | collective-permute-start | bytes 10838024 | tf_op jit(solution)/shard_map/ppermute | solution.py:32
  20.2 84.6 %collective-permute-start.5 = (bf16[176,2688]{1,0:T(8,128)(2,1)}, bf16[176,2688]{1,0:T(8,128)(2,1)}, u32[]{:S(2)}, u32[]{:S(2)}) collective-permute-start(bf16[176,2688]{1,0:T(8,128)(2,1)} %get-tuple-element.10), channel_id=1, source_target_pairs={{0,2},{1,3},{4,6},{5,7},{8,10},{9,11},{12,14},{13,15},{16,18},{17,... | collective-permute-start | bytes 2838536 | tf_op jit(solution)/shard_map/ppermute | solution.py:32
  22.6 82.2 %collective-permute-start.7 = (bf16[176,2688]{1,0:T(8,128)(2,1)}, bf16[176,2688]{1,0:T(8,128)(2,1)}, u32[]{:S(2)}, u32[]{:S(2)}) collective-permute-start(bf16[176,2688]{1,0:T(8,128)(2,1)} %get-tuple-element.9), channel_id=1, source_target_pairs={{0,130},{1,131},{4,134},{5,135},{8,138},{9,139},{12,142},{13,143},... | collective-permute-start | bytes 2838536 | tf_op jit(solution)/shard_map/ppermute | solution.py:32
  49.1 119.7 %all-to-all-start.1 = ((bf16[16,128,672]{1,2,0:T(8,128)(2,1)}), bf16[16,128,672]{1,2,0:T(8,128)(2,1)}, u32[]{:S(2)}, u32[]{:S(2)}) async-start(bf16[16,128,672]{1,2,0:T(8,128)(2,1)} %bitcast.33), calls=%async_computation.1 | async-start | bytes 5505024 | tf_op jit(solution)/shard_map/all_to_all | solution.py:190
  56.2 48.0 %collective-permute-start.1 = (bf16[160,2688]{1,0:T(8,128)(2,1)S(1)}, bf16[160,2688]{1,0:T(8,128)(2,1)}, u32[]{:S(2)}, u32[]{:S(2)}) collective-permute-start(bf16[160,2688]{1,0:T(8,128)(2,1)S(1)} %get-tuple-element.12), channel_id=1, source_target_pairs={{0,2},{1,3},{4,6},{5,7},{8,10},{9,11},{12,14},{13,15},{16,18},{17,... | collective-permute-start | bytes 2580488 | tf_op jit(solution)/shard_map/ppermute | solution.py:32
  56.6 47.7 %collective-permute-start.3 = (bf16[160,2688]{1,0:T(8,128)(2,1)S(1)}, bf16[160,2688]{1,0:T(8,128)(2,1)}, u32[]{:S(2)}, u32[]{:S(2)}) collective-permute-start(bf16[160,2688]{1,0:T(8,128)(2,1)S(1)} %get-tuple-element.11), channel_id=1, source_target_pairs={{0,130},{1,131},{4,134},{5,135},{8,138},{9,139},{12,142},{13,143},... | collective-permute-start | bytes 2580488 | tf_op jit(solution)/shard_map/ppermute | solution.py:32
  104.3 4.7 %collective-permute-start.2 = (bf16[160,2688]{1,0:T(8,128)(2,1)}, bf16[160,2688]{1,0:T(8,128)(2,1)}, u32[]{:S(2)}, u32[]{:S(2)}) collective-permute-start(bf16[160,2688]{1,0:T(8,128)(2,1)} %collective-permute-done.1.refs_2_), channel_id=1, source_target_pairs={{0,1},{1,0},{4,5},{5,4},{8,9},{9,8},{12,13},{13,12},{16,17},{17,16... | collective-permute-start | bytes 2580488 | tf_op jit(solution)/shard_map/ppermute | solution.py:32
  104.3 4.7 %collective-permute-start.4 = (bf16[160,2688]{1,0:T(8,128)(2,1)}, bf16[160,2688]{1,0:T(8,128)(2,1)}, u32[]{:S(2)}, u32[]{:S(2)}) collective-permute-start(bf16[160,2688]{1,0:T(8,128)(2,1)} %collective-permute-done.3.refs_4_), channel_id=1, source_target_pairs={{0,1},{1,0},{4,5},{5,4},{8,9},{9,8},{12,13},{13,12},{16,17},{17,16... | collective-permute-start | bytes 2580488 | tf_op jit(solution)/shard_map/ppermute | solution.py:32
  104.8 4.8 %collective-permute-start.6 = (bf16[176,2688]{1,0:T(8,128)(2,1)}, bf16[176,2688]{1,0:T(8,128)(2,1)}, u32[]{:S(2)}, u32[]{:S(2)}) collective-permute-start(bf16[176,2688]{1,0:T(8,128)(2,1)} %collective-permute-done.5.refs_6_), channel_id=1, source_target_pairs={{0,1},{1,0},{4,5},{5,4},{8,9},{9,8},{12,13},{13,12},{16,17},{17,16... | collective-permute-start | bytes 2838536 | tf_op jit(solution)/shard_map/ppermute | solution.py:32
  104.9 6.1 %collective-permute-start.8 = (bf16[176,2688]{1,0:T(8,128)(2,1)}, bf16[176,2688]{1,0:T(8,128)(2,1)}, u32[]{:S(2)}, u32[]{:S(2)}) collective-permute-start(bf16[176,2688]{1,0:T(8,128)(2,1)} %collective-permute-done.7.refs_8_), channel_id=1, source_target_pairs={{0,1},{1,0},{4,5},{5,4},{8,9},{9,8},{12,13},{13,12},{16,17},{17,16... | collective-permute-start | bytes 2838536 | tf_op jit(solution)/shard_map/ppermute | solution.py:32
  107.8 4.5 %copy-start = (f32[128,2688]{1,0:T(8,128)}, f32[128,2688]{1,0:T(8,128)S(1)}, u32[]{:S(2)}) copy-start(f32[128,2688]{1,0:T(8,128)S(1)} %reshape.116.refs_11_) | copy-start | bytes 4128772
  168.8 60.2 %all-to-all-start.2 = ((bf16[16,144,672]{2,1,0:T(8,128)(2,1)}), bf16[16,144,672]{2,1,0:T(8,128)(2,1)S(1)}, u32[]{:S(2)}, u32[]{:S(2)}) async-start(bf16[16,144,672]{2,1,0:T(8,128)(2,1)} %bitcast.9), calls=%async_computation.2 | async-start | bytes 7077888 | tf_op jit(solution)/shard_map/all_to_all | solution.py:218
  278.7 1.6 copy-start.2
